TPU v7x, 128 devices: a whole 4x4x4 slice. The times are simulated.
128 devices in a mesh: fsdp: 32 (over y, x, core), own: 4 (over z).
Axes of the slice: x: 4, y: 4, z: 4, core: 2. Of those that a mesh axis runs over, the one named last changes fastest.
Arguments:
- gradients: bfloat16 [64, 512, 512], P('own', 'fsdp'), may hold values from -120 to 120
- old_stats: float32 [256, 512, 512], P(('fsdp', 'own')), may hold values from -0.25 to 1536, as said below
- stat_slot: int32 [128], replicated, may hold values from 0 to 255, as said below
Outputs:
- update: bfloat16 [64, 512, 512], P('own', 'fsdp')
- new_stats: float32 [256, 512, 512], P(('fsdp', 'own'))
Inputs may be any that keep to these rules, and one draw needn't show every extreme that they name: `stat_slot`: statistics 2b and 2b+1 belong to block b, and block b lies on own index b // 16. Every statistic has a slot of its own; slot g lies on device g // 2, devices numbered with fsdp slowest. The statistics of the blocks of own index j lie in slots of devices with own index (j + 2) mod 4. Some device holds 2 statistics. `old_stats`: every slot is symmetric, and each diagonal entry exceeds the sum of the magnitudes of the other entries of its row.
All inputs are finite; a program needn't handle non-finite values.
Results may differ from a plain program's by a relative error of at most 0.0071.
Values may be sent and summed in bfloat16 or wider, within the bound.
A program may use at most 128 MiB of HBM per device.

v0:
```python
import jax
import jax.numpy as jnp
from jax import lax
from jax.sharding import PartitionSpec as P

ITERS = 6


keep_weight = 0.9
fresh_weight = 0.1
graft_eps = 1e-06


def passed_along(block, axis, distance):
    devices = range(lax.axis_size(axis))
    route = [((i - distance) % len(devices), i) for i in devices]
    return lax.ppermute(block, axis, route)


def batched_product(left_side, right_side):
    return jnp.einsum("cab,cbd->cad", left_side, right_side, precision=lax.Precision.HIGHEST)


def inverse_roots(matrices):
    block_width = matrices.shape[1]
    identity = jnp.eye(block_width, dtype=jnp.float32)[None]
    trace_value = jnp.sum(matrices * identity, axis=(1, 2))[:, None, None]
    moment = matrices / trace_value
    inverse = identity * trace_value ** (-0.25)
    for sweep in range(ITERS):
        factor = (5.0 * identity - moment) * 0.25
        inverse = batched_product(inverse, factor)
        square = batched_product(factor, factor)
        moment = batched_product(square, batched_product(square, moment))
    return inverse


def body(gradients, old_stats, stat_slot):
    fsdp_count = lax.axis_size("fsdp")
    own_count = lax.axis_size("own")
    half_axis = own_count // 2
    blk_count, row_count, block_width = gradients.shape
    slot_count = old_stats.shape[0]
    col_stats = 2 * blk_count
    row_index = lax.axis_index("fsdp")
    col_index = lax.axis_index("own")
    self_index = row_index * own_count + col_index
    fsdp_ids = jnp.arange(fsdp_count, dtype=jnp.int32)
    cap_ids = jnp.arange(slot_count, dtype=jnp.int32)
    blk_ids = jnp.arange(blk_count, dtype=jnp.int32)
    local_ids = jnp.arange(col_stats, dtype=jnp.int32)
    stat_ids = jnp.arange(stat_slot.shape[0], dtype=jnp.int32)

    def column_owners(column):
        slots = lax.dynamic_slice_in_dim(stat_slot, column * col_stats, col_stats)
        return (slots // slot_count // own_count, slots % slot_count)

    owner_row, owner_cap = column_owners(col_index)
    hits = (
        (owner_cap[:, None, None, None] == cap_ids[None, :, None, None])
        & (owner_row[:, None, None, None] == fsdp_ids[None, None, :, None])
        & ((local_ids // 2)[:, None, None, None] == blk_ids[None, None, None, :])
    )
    outgoing = jnp.einsum(
        "cik,krx->cirx",
        jnp.any(hits, axis=0).astype(jnp.bfloat16),
        gradients,
        preferred_element_type=jnp.bfloat16,
    )
    exchanged = lax.all_to_all(outgoing, "fsdp", split_axis=1, concat_axis=1, tiled=True)
    received = passed_along(exchanged, "own", half_axis)
    blocks = received.reshape(slot_count, fsdp_count * row_count, block_width)
    my_slots = self_index * slot_count + cap_ids
    slot_match = stat_slot[None, :] == my_slots[:, None]
    mine_used = jnp.any(slot_match, axis=1)
    mine_stat = jnp.sum(jnp.where(slot_match, stat_ids[None, :], 0), axis=1)
    mine_side = mine_stat % 2
    oriented = jnp.where((mine_side == 1)[:, None, None], jnp.swapaxes(blocks, 1, 2), blocks)
    gram_matrix = jnp.einsum("cab,cdb->cad", oriented, oriented, preferred_element_type=jnp.float32)
    updated = keep_weight * old_stats + fresh_weight * gram_matrix
    new_stats = jnp.where(mine_used[:, None, None], updated, old_stats)
    roots = inverse_roots(new_stats).astype(jnp.bfloat16)
    sendable = jnp.where((mine_side == 0)[:, None, None], jnp.swapaxes(roots, 1, 2), roots)
    pieces = sendable.reshape(slot_count, fsdp_count, row_count, block_width)
    returned = lax.all_to_all(pieces, "fsdp", split_axis=1, concat_axis=1, tiled=True)
    returned = passed_along(returned, "own", half_axis)
    owner_row, owner_cap = column_owners(col_index)
    combined = owner_cap * fsdp_count + owner_row
    source_ids = jnp.arange(slot_count * fsdp_count, dtype=jnp.int32)
    owner_pick = (combined[:, None] == source_ids[None, :]).astype(jnp.bfloat16)
    flat_back = returned.reshape(slot_count * fsdp_count, row_count, block_width)
    mine_roots = jnp.einsum(
        "tq,qrx->trx", owner_pick, flat_back, preferred_element_type=jnp.float32
    ).astype(jnp.bfloat16)
    mine_roots = mine_roots.reshape(blk_count, 2, row_count, block_width)
    left_rows = mine_roots[:, 0]
    right_rows = mine_roots[:, 1]
    mixed = lax.psum_scatter(
        jnp.einsum("kra,krx->akx", left_rows, gradients, preferred_element_type=jnp.float32),
        "fsdp",
        scatter_dimension=0,
        tiled=True,
    )
    hidden = jnp.swapaxes(mixed, 0, 1).astype(jnp.bfloat16)
    shaped = jnp.einsum(
        "krb,kbx->krx",
        hidden,
        lax.all_gather(right_rows, "fsdp", axis=1, tiled=True),
        preferred_element_type=jnp.float32,
    )
    grad_wide = gradients.astype(jnp.float32)
    grad_squares = jnp.sum(grad_wide * grad_wide, axis=(1, 2))
    shaped_squares = jnp.sum(shaped * shaped, axis=(1, 2))
    grad_total, shaped_total = lax.psum((grad_squares, shaped_squares), "fsdp")
    ratio = jnp.sqrt(grad_total / (shaped_total + graft_eps))
    update = (shaped * ratio[:, None, None]).astype(jnp.bfloat16)
    return (update, new_stats)


def solution(mesh):
    return jax.shard_map(
        body,
        mesh=mesh,
        in_specs=(P("own", "fsdp", None), P(("fsdp", "own"), None, None), P()),
        out_specs=(P("own", "fsdp", None), P(("fsdp", "own"), None, None)),
        check_vma=False,
    )
```

profile of v0, /device:TPU:1, one launch (start us, length us, event | category | flops | bytes accessed | tf_op | source)
XLA Modules:
  0.0 444.3 jit_solution(12256315324284534697)
XLA Ops:
  11.4 8.7 %all-to-all-start = ((bf16[2,32,16,512]{3,2,0,1:T(8,128)(2,1)}), bf16[2,32,16,512]{3,2,0,1:T(8,128)(2,1)S(1)}, u32[]{:S(2)}, u32[]{:S(2)}) async-start(bf16[2,32,16,512]{3,2,0,1:T(8,128)(2,1)} %copy.27), calls=%async_computation | async-start | bytes 2097152 | tf_op jit(solution)/shard_map/all_to_all | solution.py:70
  20.2 17.1 %all-to-all-done = bf16[2,32,16,512]{3,2,0,1:T(8,128)(2,1)S(1)} async-done(((bf16[2,32,16,512]{3,2,0,1:T(8,128)(2,1)}), bf16[2,32,16,512]{3,2,0,1:T(8,128)(2,1)S(1)}, u32[]{:S(2)}, u32[]{:S(2)}) %all-to-all-start) | async-done | bytes 1048608 | tf_op jit(solution)/shard_map/all_to_all | solution.py:70
  37.4 3.7 collective-permute-start
  41.7 22.6 %collective-permute-done = bf16[2,32,16,512]{3,2,1,0:T(8,128)(2,1)S(1)} collective-permute-done((bf16[2,32,16,512]{3,2,1,0:T(8,128)(2,1)S(1)}, bf16[2,32,16,512]{3,2,1,0:T(8,128)(2,1)S(1)}, u32[]{:S(2)}, u32[]{:S(2)}) %collective-permute-start) | collective-permute-done | bytes 1048608 | tf_op jit(solution)/shard_map/ppermute | solution.py:17
  69.6 4.0 fusion.7
  73.6 3.7 fusion.69
  80.8 3.9 fusion.8
  91.8 3.7 fusion.10
  95.6 3.8 fusion.74
  102.9 3.7 fusion.12
  110.2 3.9 fusion.77
  114.1 3.7 fusion.14
  121.4 3.7 fusion.79
  125.1 3.9 fusion.5
  132.7 3.7 fusion.11
  136.4 3.9 fusion.13
  140.3 3.7 fusion.15
  148.5 20.9 %all_to_all.10 = bf16[2,32,16,512]{3,2,0,1:T(8,128)(2,1)S(1)} all-to-all(bf16[2,32,16,512]{3,2,0,1:T(8,128)(2,1)S(1)} %copy.31), channel_id=1, replica_groups=mesh['fsdp'=32,'own'=4] {'fsdp'}, dimensions={1} | all-to-all | bytes 2097152 | tf_op jit(solution)/shard_map/all_to_all | solution.py:85
  172.7 23.2 %collective-permute-done.1 = bf16[2,32,16,512]{3,2,0,1:T(8,128)(2,1)S(1)} collective-permute-done((bf16[2,32,16,512]{3,2,0,1:T(8,128)(2,1)S(1)}, bf16[2,32,16,512]{3,2,0,1:T(8,128)(2,1)S(1)}, u32[]{:S(2)}, u32[]{:S(2)}) %collective-permute-start.1) | collective-permute-done | bytes 1048608 | tf_op jit(solution)/shard_map/ppermute | solution.py:17
  199.2 8.1 %convolution_bitcast_fusion = f32[512,16,512]{2,0,1:T(8,128)} fusion(bf16[16,16,512]{2,1,0:T(8,128)(2,1)S(1)} %copy-done, bf16[16,1,16,512]{3,1,0,2:T(2,128)(2,1)S(1)} %get-tuple-element.9), kind=kOutput, calls=%fused_computation | convolution fusion | flops 134217728 | bytes 17301504 | tf_op jit(solution)/shard_map/kra,krx->akx/dot_general | solution.py:99
  207.6 43.0 %all-gather.3.cloned.1.call-done = bf16[16,1,512,512]{3,2,0,1:T(8,128)(2,1)} async-done(((bf16[16,1,16,512]{3,2,0,1:T(8,128)(2,1)}), bf16[16,1,512,512]{3,2,0,1:T(8,128)(2,1)}) %all-gather.3.cloned.1.call-update) | async-done | bytes 8388624 | tf_op jit(solution)/shard_map/all_gather | solution.py:108
  250.6 116.8 %reduce-scatter.2.cloned.1.call-done = f32[16,16,512]{2,0,1:T(8,128)} async-done(((f32[512,16,512]{2,0,1:T(8,128)}), f32[16,16,512]{2,0,1:T(8,128)}) %reduce-scatter.2.cloned.1.call-update) | async-done | bytes 524304 | tf_op jit(solution)/shard_map/reduce_scatter | solution.py:98
  367.4 4.9 %multiply_reduce_fusion.1 = (f32[16]{0:T(128)S(1)}, f32[16,16,512]{2,1,0:T(8,128)S(1)}) fusion(bf16[16,1,512,512]{3,2,0,1:T(8,128)(2,1)} %all-gather.3.cloned.1.call-done, f32[16,16,512]{2,0,1:T(8,128)} %reduce-scatter.2.cloned.1.call-done), kind=kOutput, calls=%fused_computation.58 | convolution fusion | flops 134610928 | bytes 9437248 | tf_op jit(solution)/shard_map/krb,kbx->krx/dot_general | solution.py:105
  372.3 64.1 %all-reduce = (f32[16]{0:T(128)S(1)}, f32[16]{0:T(128)S(1)}) all-reduce(f32[16]{0:T(128)S(1)} %multiply_reduce_fusion.2, f32[16]{0:T(128)S(1)} %get-tuple-element.13), channel_id=1, replica_groups=mesh['fsdp'=32,'own'=4] {'fsdp'}, use_global_device_ids=true, to_apply=%region_6.7 | all-reduce | flops 32 | bytes 256 | tf_op jit(solution)/shard_map/psum | solution.py:114
  (50 shorter events, 47.1 us)
Async XLA Ops:
  11.4 29.7 %copy-start.2 = (s32[128]{0:T(128)S(1)}, s32[128]{0:T(128)}, u32[]{:S(2)}) copy-start(s32[128]{0:T(128)} %param.5) | copy-start | bytes 1540
  11.4 25.9 %all-to-all-start = ((bf16[2,32,16,512]{3,2,0,1:T(8,128)(2,1)}), bf16[2,32,16,512]{3,2,0,1:T(8,128)(2,1)S(1)}, u32[]{:S(2)}, u32[]{:S(2)}) async-start(bf16[2,32,16,512]{3,2,0,1:T(8,128)(2,1)} %copy.27), calls=%async_computation | async-start | bytes 2097152 | tf_op jit(solution)/shard_map/all_to_all | solution.py:70
  20.1 230.5 %all-gather.3.cloned.1.call-start = ((), (), s32[]{:S(2)}) async-start(), calls=%async_computation.4 | async-start | bytes 8650752 | tf_op jit(solution)/shard_map/all_gather | solution.py:108
  37.4 26.9 %collective-permute-start = (bf16[2,32,16,512]{3,2,1,0:T(8,128)(2,1)S(1)}, bf16[2,32,16,512]{3,2,1,0:T(8,128)(2,1)S(1)}, u32[]{:S(2)}, u32[]{:S(2)}) collective-permute-start(bf16[2,32,16,512]{3,2,1,0:T(8,128)(2,1)S(1)} %copy.28), channel_id=1, source_target_pairs={{2,0},{3,1},{0,2},{1,3},{6,4},{7,5},{4,6},{5,7},{10,8},{11,9},{8,1... | collective-permute-start | bytes 3145736 | tf_op jit(solution)/shard_map/ppermute | solution.py:17
  69.6 55.5 %copy-start.1 = (f32[2,512,512]{2,1,0:T(8,128)}, f32[2,512,512]{2,1,0:T(8,128)S(1)}, u32[]{:S(2)}) copy-start(f32[2,512,512]{2,1,0:T(8,128)S(1)} %get-tuple-element.12) | copy-start | bytes 6291460
  169.4 26.5 %collective-permute-start.1 = (bf16[2,32,16,512]{3,2,0,1:T(8,128)(2,1)S(1)}, bf16[2,32,16,512]{3,2,0,1:T(8,128)(2,1)S(1)}, u32[]{:S(2)}, u32[]{:S(2)}) collective-permute-start(bf16[2,32,16,512]{3,2,0,1:T(8,128)(2,1)S(1)} %all_to_all.10), channel_id=1, source_target_pairs={{2,0},{3,1},{0,2},{1,3},{6,4},{7,5},{4,6},{5,7},{10,8},{11,9},{8,1... | collective-permute-start | bytes 3145736 | tf_op jit(solution)/shard_map/ppermute | solution.py:17
  196.9 2.3 copy-start
  198.9 168.5 %reduce-scatter.2.cloned.1.call-start = ((), (), s32[]{:S(2)}) async-start(), calls=%async_computation.3 | async-start | bytes 17301504 | tf_op jit(solution)/shard_map/reduce_scatter | solution.py:98
Sparse Core Ops, SparseCore 0:
  199.0 51.5 all-gather.2
  254.5 112.8 reduce-scatter.1
where the time goes:
time: 447 us; the launch traced here: 444 us
  waiting for transfers between devices  223 us (50%)
  matrix products  96.2 us (22%)
  blocking collectives  85 us (19%)
  starting transfers between devices  16 us (4%)
  between operations  14.6 us (3%)
  local copies, waits for them, and re-layouts  6.63 us (1%)
    reduce_scatter x1, waiting for transfers between devices, body(): lax.psum_scatter(jnp.einsum('kra,krx->akx', left_rows, gradients, preferr...  117 us
    dot_general x21, matrix products, batched_product(): jnp.einsum('cab,cbd->cad', left_side, right_side, precision=lax.Precision...  77.9 us
    psum x1, blocking collectives, body(): grad_total, shaped_total = lax.psum((grad_squares, shaped_squares), 'fsdp')  64.1 us
    ppermute x2, waiting for transfers between devices, passed_along(): return lax.ppermute(block, axis, route)  45.8 us
    all_gather x1, waiting for transfers between devices, body(): lax.all_gather(right_rows, 'fsdp', axis=1, tiled=True)  43 us
    all_to_all x1, blocking collectives, body(): lax.all_to_all(pieces, 'fsdp', split_axis=1, concat_axis=1, tiled=True)  20.9 us
    all_to_all x1, waiting for transfers between devices, body(): lax.all_to_all(outgoing, 'fsdp', split_axis=1, concat_axis=1, tiled=True)  17.1 us
  transfers between devices with their start and end apart: 5, of which 5 were waited for; matrix products, arithmetic and copies ran while one was open for 2% of the time, Pallas kernels for 0%

commit v1 on v0

v1 whole, which is shorter than its diff:
```python
import functools

import jax
import jax.numpy as jnp
from jax import lax
from jax.experimental import pallas as pl
from jax.experimental.pallas import tpu as pltpu
from jax.sharding import PartitionSpec as P

ITERS = 6
CAPS = 2

keep_weight = 0.9
fresh_weight = 0.1
graft_eps = 1e-06

MESH = pl.DeviceIdType.MESH
BF16 = jnp.bfloat16
F32 = jnp.float32


def product(left_side, right_side):
    return jnp.dot(left_side, right_side, preferred_element_type=F32)


def rows_gram(block):
    return lax.dot_general(block, block, (((1,), (1,)), ((), ())), preferred_element_type=F32)


def columns_gram(block):
    return lax.dot_general(block, block, (((0,), (0,)), ((), ())), preferred_element_type=F32)


def total(values):
    return jnp.sum(jnp.sum(values, axis=0, keepdims=True), axis=1, keepdims=True)


def diagonal_mask(width):
    rows = lax.broadcasted_iota(jnp.int32, (width, width), 0)
    return rows == lax.broadcasted_iota(jnp.int32, (width, width), 1)


def kernel(
    slot_ref, table_ref, grad_ref, old_ref,
    update_ref, new_ref,
    old_wide, spread, gathered, chosen, old_rows, far_rows, block_rows,
    routed, routed_in, roots, moment, moment_low, gap_low, mixed_low, inverse, out_rows,
    load_sem, local_sem, send_sems, recv_sems,
):
    fsdp_count = spread.shape[0]
    own_count = lax.axis_size("own")
    chip_count = fsdp_count // 2
    row_count, width = grad_ref.shape[1:]
    f = lax.axis_index("fsdp")
    q = lax.axis_index("own")
    far = lax.rem(q + own_count // 2, own_count)
    core = lax.rem(f, 2)
    chip = f // 2
    sibling = f + 1 - 2 * core

    def peer(d):
        return lax.rem(f + d, fsdp_count)

    def push(src, dst, phase, row, plane):
        return pltpu.make_async_remote_copy(
            src_ref=src,
            dst_ref=dst,
            send_sem=send_sems.at[phase],
            recv_sem=recv_sems.at[phase],
            device_id={"fsdp": row, "own": plane},
            device_id_type=MESH,
        )

    def arrived(ref, phase):
        pltpu.make_async_copy(ref, ref, recv_sems.at[phase]).wait()

    def left_here(ref, phase):
        pltpu.make_async_copy(ref, ref, send_sems.at[phase]).wait()

    loads = [
        pltpu.make_async_copy(old_ref.at[c], old_wide.at[c], load_sem.at[c]) for c in range(CAPS)
    ]
    for load in loads:
        load.start()

    barrier = pltpu.get_barrier_semaphore()

    @pl.loop(1, fsdp_count)
    def _(d):
        pl.semaphore_signal(
            barrier, inc=1, device_id={"fsdp": peer(d), "own": q}, device_id_type=MESH
        )

    @pl.loop(0, fsdp_count)
    def _(d):
        pl.semaphore_signal(
            barrier, inc=1, device_id={"fsdp": peer(d), "own": far}, device_id_type=MESH
        )

    for c in range(CAPS):
        loads[c].wait()

        @pl.loop(0, fsdp_count)
        def _(r):
            rows = pl.ds(pl.multiple_of(r * row_count, row_count), row_count)
            spread[r, c] = old_wide[c, rows, :].astype(BF16)

    pl.semaphore_wait(barrier, 2 * fsdp_count - 1)

    @pl.loop(1, fsdp_count)
    def _(d):
        t = peer(d)
        push(spread.at[t], gathered.at[f], 0, t, q).start()

    own_spread = pltpu.make_async_copy(spread.at[f], gathered.at[f], recv_sems.at[0])
    own_spread.start()

    far_push = push(grad_ref, far_rows, 1, f, far)
    far_push.start()

    @pl.loop(1, chip_count)
    def _(d):
        t = lax.rem(chip + d, chip_count)
        push(grad_ref.at[t], block_rows.at[chip, core], 2, 2 * t + core, q).start()

    pltpu.make_async_copy(grad_ref.at[chip], block_rows.at[chip, core], recv_sems.at[2]).start()
    arrived(block_rows.at[:, core], 2)
    swap = push(block_rows.at[:, core], block_rows.at[:, core], 3, sibling, q)
    swap.start()

    arrived(gathered, 0)

    @pl.loop(0, fsdp_count)
    def _(d):
        t = peer(d)
        slot = slot_ref[far * fsdp_count + t]
        chosen[t] = gathered[slot // (CAPS * own_count), lax.rem(slot, CAPS)]
        push(chosen.at[t], old_rows.at[f], 4, t, far).start()

    far_push.wait_recv()

    def choose(t):
        for c in range(CAPS):
            entry = table_ref[t * CAPS + c]
            routed[t, c] = far_rows[lax.max(entry - 1, 0) // 2]

    @pl.loop(1, fsdp_count)
    def _(d):
        t = peer(d)
        choose(t)
        push(routed.at[t], routed_in.at[f], 5, t, q).start()

    choose(f)
    pltpu.make_async_copy(routed.at[f], routed_in.at[f], recv_sems.at[5]).start()

    swap.wait()
    block = block_rows[...].reshape(width, width)
    wide = block.astype(F32)
    grad_total = total(wide * wide)

    @pl.when(core == 0)
    def _():
        moment[...] = rows_gram(block)

    @pl.when(core == 1)
    def _():
        moment[...] = columns_gram(block)

    arrived(old_rows, 4)
    on_diagonal = diagonal_mask(width)
    statistic = keep_weight * old_rows[...].reshape(width, width).astype(F32) + (
        fresh_weight * moment[...]
    )
    trace_value = total(jnp.where(on_diagonal, statistic, 0.0))
    start = statistic * (1.0 / trace_value)
    moment[...] = start
    moment_low[...] = start.astype(BF16)
    inverse[...] = -0.25 * start

    def sweep(step, level):
        low = moment_low[...]
        gap_low[...] = (product(low, low) - 10.0 * moment[...]).astype(BF16)
        mixed = (25.0 * moment[...] + product(gap_low[...], low)) * (1.0 / 16.0)
        mixed_low[...] = mixed.astype(BF16)
        fresh = (25.0 * mixed + product(gap_low[...], mixed_low[...])) * (1.0 / 16.0)
        moment[...] = fresh
        moment_low[...] = fresh.astype(BF16)
        inverse[...] = 1.25 * inverse[...] - 0.25 * (
            level * fresh + product(inverse[...].astype(BF16), moment_low[...])
        )
        return level * 1.25

    level = lax.fori_loop(0, ITERS - 1, sweep, jnp.float32(1.25))
    scale = 1.0 / jnp.sqrt(jnp.sqrt(trace_value))
    root = (jnp.where(on_diagonal, level, 0.0) + inverse[...]) * scale
    roots[core] = root.astype(BF16)
    trade = push(roots.at[core], roots.at[core], 6, sibling, q)
    trade.start()
    trade.wait()

    hidden = product(roots[0], block).astype(BF16)
    shaped = product(hidden, roots[1])
    ratio = jnp.sqrt(grad_total / (total(shaped * shaped) + graft_eps))
    out_rows[...] = (shaped * ratio).astype(BF16).reshape(out_rows.shape)

    @pl.loop(1, chip_count)
    def _(d):
        t = lax.rem(chip + d, chip_count)
        push(out_rows.at[t, core], update_ref.at[chip], 7, 2 * t + core, q).start()

    pltpu.make_async_copy(out_rows.at[chip, core], update_ref.at[chip], recv_sems.at[7]).start()

    arrived(routed_in, 5)
    for c in range(CAPS):
        entry = table_ref[f * CAPS + c]
        used = entry > 0
        odd = lax.rem(lax.max(entry - 1, 0), 2) == 1
        keep = jnp.where(used, keep_weight, 1.0)
        fresh = jnp.where(used, fresh_weight, 0.0)
        fresh_right = jnp.where(odd, fresh, 0.0)
        source = routed_in[:, c].reshape(width, width)
        gram = (fresh - fresh_right) * rows_gram(source) + fresh_right * columns_gram(source)
        old_wide[c] = keep * old_wide[c] + gram
        pltpu.make_async_copy(old_wide.at[c], new_ref.at[c], load_sem.at[c]).start()

    for c in range(CAPS):
        pltpu.make_async_copy(old_wide.at[c], new_ref.at[c], load_sem.at[c]).wait()
    arrived(update_ref, 7)

    left_here(spread.at[pl.ds(0, fsdp_count - 1)], 0)
    far_push.wait_send()
    left_here(grad_ref.at[pl.ds(0, chip_count - 1)], 2)
    left_here(chosen, 4)
    left_here(routed.at[pl.ds(0, fsdp_count - 1)], 5)
    left_here(out_rows.at[pl.ds(0, chip_count - 1), 0], 7)


def body(gradients, old_stats, stat_slot):
    fsdp_count = lax.axis_size("fsdp")
    own_count = lax.axis_size("own")
    blk_count, row_count, width = gradients.shape
    far = (lax.axis_index("own") + own_count // 2) % own_count
    slots = lax.dynamic_slice_in_dim(stat_slot, far * fsdp_count, fsdp_count)
    places = slots // (CAPS * own_count) * CAPS + slots % CAPS
    place_ids = jnp.arange(fsdp_count * CAPS, dtype=jnp.int32)
    stat_ids = jnp.arange(1, fsdp_count + 1, dtype=jnp.int32)
    table = jnp.sum(
        jnp.where(places[None, :] == place_ids[:, None], stat_ids[None, :], 0), axis=1
    ).astype(jnp.int32)

    square = (width, width)
    vmem = pltpu.VMEM
    return pl.pallas_call(
        kernel,
        out_shape=(
            jax.ShapeDtypeStruct(gradients.shape, gradients.dtype),
            jax.ShapeDtypeStruct(old_stats.shape, old_stats.dtype),
        ),
        in_specs=[
            pl.BlockSpec(memory_space=pltpu.SMEM),
            pl.BlockSpec(memory_space=pltpu.SMEM),
            pl.BlockSpec(memory_space=pl.ANY),
            pl.BlockSpec(memory_space=pl.ANY),
        ],
        out_specs=(pl.BlockSpec(memory_space=pl.ANY), pl.BlockSpec(memory_space=pl.ANY)),
        scratch_shapes=[
            vmem((CAPS, *square), F32),
            vmem((fsdp_count, CAPS, row_count, width), BF16),
            vmem((fsdp_count, CAPS, row_count, width), BF16),
            vmem((fsdp_count, row_count, width), BF16),
            vmem((fsdp_count, row_count, width), BF16),
            vmem((blk_count, row_count, width), BF16),
            vmem((fsdp_count // 2, 2, row_count, width), BF16),
            vmem((fsdp_count, CAPS, row_count, width), BF16),
            vmem((fsdp_count, CAPS, row_count, width), BF16),
            vmem((2, *square), BF16),
            vmem(square, F32),
            vmem(square, BF16),
            vmem(square, BF16),
            vmem(square, BF16),
            vmem(square, F32),
            vmem((fsdp_count // 2, 2, row_count, width), BF16),
            pltpu.SemaphoreType.DMA((CAPS,)),
            pltpu.SemaphoreType.DMA((1,)),
            pltpu.SemaphoreType.DMA((8,)),
            pltpu.SemaphoreType.DMA((8,)),
        ],
        compiler_params=pltpu.CompilerParams(
            collective_id=0, has_side_effects=True, vmem_limit_bytes=48 * 2**20
        ),
        cost_estimate=pl.CostEstimate(
            flops=60 * width**3, bytes_accessed=5 * 2**20, transcendentals=0
        ),
    )(stat_slot, table, gradients, old_stats)


def solution(mesh):
    return jax.shard_map(
        body,
        mesh=mesh,
        in_specs=(P("own", "fsdp", None), P(("fsdp", "own"), None, None), P()),
        out_specs=(P("own", "fsdp", None), P(("fsdp", "own"), None, None)),
        check_vma=False,
    )
```

time: 447 us -> 71.9 us (0.16)
  waiting for transfers between devices: 223 us -> 0 us
  matrix products: 96.2 us -> 0 us
  blocking collectives: 85 us -> 0 us
  Pallas kernels: 0 us -> 65 us
  starting transfers between devices: 16 us -> 0 us
  between operations: 14.6 us -> 0.66 us
    reduce_scatter x1 -> x0, waiting for transfers between devices: 117 us -> none  [body(): lax.psum_scatter(jnp.einsum('kra,krx->akx', left_rows, gradients, preferr...]
    dot_general x26 -> x0, matrix products: 96.2 us -> none  [the longest x21 77.9 us: batched_product(): jnp.einsum('cab,cbd->cad', left_side, right_side, precision=lax.Precision...]
    pallas_call x0 -> x1, Pallas kernels: none -> 65 us  [body(): pl.pallas_call(kernel, out_shape=(jax.ShapeDtypeStruct(gradients.shape, g...]
    psum x1 -> x0, blocking collectives: 64.1 us -> none  [body(): grad_total, shaped_total = lax.psum((grad_squares, shaped_squares), 'fsdp')]
    ppermute x2 -> x0, waiting for transfers between devices: 45.8 us -> none  [passed_along(): return lax.ppermute(block, axis, route)]
    all_gather x1 -> x0, waiting for transfers between devices: 43 us -> none  [body(): lax.all_gather(right_rows, 'fsdp', axis=1, tiled=True)]
    all_to_all x1 -> x0, blocking collectives: 20.9 us -> none  [body(): lax.all_to_all(pieces, 'fsdp', split_axis=1, concat_axis=1, tiled=True)]
    all_to_all x1 -> x0, waiting for transfers between devices: 17.1 us -> none  [body(): lax.all_to_all(outgoing, 'fsdp', split_axis=1, concat_axis=1, tiled=True)]
  transfers between devices with their start and end apart: 5 -> 0, of which waited for: 5 -> 0; matrix products, arithmetic and copies ran while one was open for 2% -> 0% of each run, Pallas kernels for 0% -> 0%
where the time goes in v1:
time: 71.9 us; the launch traced here: 71.7 us
  Pallas kernels  65 us (90%)
  local copies, waits for them, and re-layouts  5.21 us (7%)
  other arithmetic  0.84 us (1%)
    pallas_call x1, Pallas kernels, body(): pl.pallas_call(kernel, out_shape=(jax.ShapeDtypeStruct(gradients.shape, g...  65 us
    unnamed x8, local copies, waits for them, and re-layouts  5.21 us

profile of v1, /device:TPU:1, one launch (start us, length us, event | category | flops | bytes accessed | tf_op | source)
XLA Modules:
  0.0 71.7 jit_solution(15366936521836633136)
XLA Ops:
  0.6 0.7 %fusion = (s32[32]{0:T(128)S(1)}, s32[32]{0:T(128)S(1)}) fusion(s32[128]{0:T(128)} %slot_ref.1, s32[]{:T(128)S(6)} %select_n.26), kind=kLoop, calls=%fused_computation.8 | loop fusion | flops 832 | bytes 388 | tf_op jit(solution)/shard_map/add | solution.py:244
  1.4 0.1 select_reduce_fusion.table_ref
  1.5 0.0 copy-start
  1.5 0.6 copy-done
  2.1 0.0 copy-start.1
  2.1 1.6 %copy-done.1 = f32[2,512,512]{2,1,0:T(8,128)S(1)} copy-done((f32[2,512,512]{2,1,0:T(8,128)S(1)}, f32[2,512,512]{2,1,0:T(8,128)}, u32[]{:S(2)}) %copy-start.1) | copy-done | bytes 2097176
  3.7 0.0 copy-start.2
  3.7 0.9 %copy-done.2 = bf16[16,16,512]{2,1,0:T(8,128)(2,1)S(1)} copy-done((bf16[16,16,512]{2,1,0:T(8,128)(2,1)S(1)}, bf16[16,16,512]{2,1,0:T(8,128)(2,1)}, u32[]{:S(2)}) %copy-start.2) | copy-done | bytes 262168
  4.7 65.0 %shard_map.50 = (bf16[16,16,512]{2,1,0:T(8,128)(2,1)S(1)}, f32[2,512,512]{2,1,0:T(8,128)S(1)}) custom-call(s32[128]{0:T(128)S(1)} %copy-done, s32[64]{0:T(128)S(1)} %select_reduce_fusion.table_ref, bf16[16,16,512]{2,1,0:T(8,128)(2,1)S(1)} %copy-done.2, f32[2,512,512]{2,1,0:T(8,128)S(1)} %copy-done.1), custom_call_target="tpu_custom_call" | custom-call | flops 8053063680 | bytes 5242880 | tf_op jit(solution)/shard_map/pallas_call | solution.py:253
  69.7 0.7 copy.7
  70.4 1.3 %copy.8 = f32[2,512,512]{2,1,0:T(8,128)} copy(f32[2,512,512]{2,1,0:T(8,128)S(1)} %get-tuple-element.7) | data formatting | bytes 4194304
Async XLA Ops:
  1.5 0.7 copy-start
  2.1 1.6 %copy-start.1 = (f32[2,512,512]{2,1,0:T(8,128)S(1)}, f32[2,512,512]{2,1,0:T(8,128)}, u32[]{:S(2)}) copy-start(f32[2,512,512]{2,1,0:T(8,128)} %old_ref.1) | copy-start | bytes 6291460
  3.7 0.9 %copy-start.2 = (bf16[16,16,512]{2,1,0:T(8,128)(2,1)S(1)}, bf16[16,16,512]{2,1,0:T(8,128)(2,1)}, u32[]{:S(2)}) copy-start(bf16[16,16,512]{2,1,0:T(8,128)(2,1)} %grad_ref.1) | copy-start | bytes 786436

commit v2 on v1

v2 whole, which is shorter than its diff:
```python
import math

import jax
import jax.numpy as jnp
from jax import lax
from jax.experimental import pallas as pl
from jax.experimental.pallas import tpu as pltpu
from jax.sharding import PartitionSpec as P

ITERS = 6
CAPS = 2
SPLIT = 4

keep_weight = 0.9
fresh_weight = 0.1
graft_eps = 1e-06

MESH = pl.DeviceIdType.MESH
BF16 = jnp.bfloat16
F32 = jnp.float32


def product(left_side, right_side):
    return jnp.dot(left_side, right_side, preferred_element_type=F32)


def rows_gram(block):
    return lax.dot_general(block, block, (((1,), (1,)), ((), ())), preferred_element_type=F32)


def columns_gram(block):
    return lax.dot_general(block, block, (((0,), (0,)), ((), ())), preferred_element_type=F32)


def total(values):
    return jnp.sum(jnp.sum(values, axis=0, keepdims=True), axis=1, keepdims=True)


def diagonal_mask(width):
    rows = lax.broadcasted_iota(jnp.int32, (width, width), 0)
    return rows == lax.broadcasted_iota(jnp.int32, (width, width), 1)


def upper_blocks(width):
    side = width // SPLIT
    pairs = [(i, j) for i in range(SPLIT) for j in range(i, SPLIT)]
    return side, [(pl.ds(i * side, side), pl.ds(j * side, side)) for i, j in pairs]


def kernel(
    slot_ref, grad_ref, old_ref,
    update_ref, new_ref,
    slots, slot_row, table_row, table,
    old_wide, spread_a, spread_b, gathered_a, gathered_b, chosen_a, chosen_b, old_rows,
    far_rows, block_rows, routed, routed_in, roots,
    moment, moment_low, gap_low, mixed_low, inverse, out_rows,
    load_sem, small_sem, send_sems, recv_sems,
):
    chip_count = spread_a.shape[0]
    fsdp_count = 2 * chip_count
    chip_side = math.isqrt(chip_count)
    own_count = lax.axis_size("own")
    row_count, width = grad_ref.shape[1:]
    stat_count = slot_ref.shape[1]
    f = lax.axis_index("fsdp")
    q = lax.axis_index("own")
    far = lax.rem(q + own_count // 2, own_count)
    core = lax.rem(f, 2)
    chip = f // 2
    sibling = f + 1 - 2 * core
    parts_a = spread_a.shape[2]
    parts_b = spread_b.shape[2]

    def chip_at(d):
        turn = lax.rem(5 * d, chip_count)
        y = lax.rem(chip // chip_side + turn // chip_side, chip_side)
        x = lax.rem(chip + turn, chip_side)
        return y * chip_side + x

    def push(src, dst, phase, row, plane):
        return pltpu.make_async_remote_copy(
            src_ref=src,
            dst_ref=dst,
            send_sem=send_sems.at[phase],
            recv_sem=recv_sems.at[phase],
            device_id={"fsdp": row, "own": plane},
            device_id_type=MESH,
        )

    def keep_here(src, dst, phase):
        pltpu.make_async_copy(src, dst, recv_sems.at[phase]).start()

    def arrived(ref, phase):
        pltpu.make_async_copy(ref, ref, recv_sems.at[phase]).wait()

    def left_here(ref, phase):
        pltpu.make_async_copy(ref, ref, send_sems.at[phase]).wait()

    loads = [
        pltpu.make_async_copy(old_ref.at[c], old_wide.at[c], load_sem.at[c]) for c in range(CAPS)
    ]
    slot_loads = [
        pltpu.make_async_copy(slot_ref, slots, small_sem.at[0]),
        pltpu.make_async_copy(slot_ref, slot_row, small_sem.at[1]),
    ]
    for load in loads + slot_loads:
        load.start()

    barrier = pltpu.get_barrier_semaphore()

    def greet(row, plane):
        pl.semaphore_signal(
            barrier, inc=1, device_id={"fsdp": row, "own": plane}, device_id_type=MESH
        )

    @pl.loop(1, fsdp_count)
    def _(d):
        greet(lax.rem(f + d, fsdp_count), q)

    greet(f, far)

    side, uppers = upper_blocks(width)
    pieces = side // row_count
    for c in range(CAPS):
        loads[c].wait()
        for b, (rows, columns) in enumerate(uppers):
            low = old_wide[c, rows, columns].astype(BF16).reshape(pieces, row_count, side)
            for piece in range(pieces):
                target, part = divmod(b * pieces + piece, parts_a + parts_b)
                if part < parts_a:
                    spread_a[target, c, part] = low[piece]
                else:
                    spread_b[target, c, part - parts_a] = low[piece]

    pl.semaphore_wait(barrier, fsdp_count)

    far_push = push(grad_ref, far_rows, 1, f, far)
    far_push.start()

    def spread_to(source, target, e):
        @pl.loop(1, chip_count)
        def _(d):
            t = chip_at(d)
            push(source.at[t], target.at[f], 0, 2 * t + e, q).start()

    @pl.when(core == 0)
    def _():
        spread_to(spread_a, gathered_a, 0)
        spread_to(spread_b, gathered_b, 1)
        push(spread_b.at[chip], gathered_b.at[f], 0, sibling, q).start()
        keep_here(spread_a.at[chip], gathered_a.at[f], 0)

    @pl.when(core == 1)
    def _():
        spread_to(spread_b, gathered_b, 1)
        spread_to(spread_a, gathered_a, 0)
        push(spread_a.at[chip], gathered_a.at[f], 0, sibling, q).start()
        keep_here(spread_b.at[chip], gathered_b.at[f], 0)

    @pl.loop(1, chip_count)
    def _(d):
        t = chip_at(d)
        push(grad_ref.at[t], block_rows.at[chip, core], 2, 2 * t + core, q).start()

    keep_here(grad_ref.at[chip], block_rows.at[chip, core], 2)

    for load in slot_loads:
        load.wait()
    grid = (stat_count, stat_count)
    by_stat = jnp.transpose(jnp.broadcast_to(slot_row[...], grid))
    place = jnp.right_shift(by_stat, 3) * CAPS + jnp.bitwise_and(by_stat, 1)
    here = jnp.bitwise_and(jnp.right_shift(by_stat, 1), 3) == q
    hit = here & (place == lax.broadcasted_iota(jnp.int32, grid, 1))
    names = lax.broadcasted_iota(jnp.int32, grid, 0) + 1
    table_row[...] = jnp.sum(jnp.where(hit, names, 0), axis=0, keepdims=True)
    table_copy = pltpu.make_async_copy(table_row, table, small_sem.at[0])
    table_copy.start()
    table_copy.wait()

    arrived(block_rows.at[:, core], 2)
    swap = push(block_rows.at[:, core], block_rows.at[:, core], 3, sibling, q)
    swap.start()

    far_push.wait_recv()

    @pl.loop(0, fsdp_count)
    def _(t):
        for c in range(CAPS):
            entry = lax.max(table[0, t * CAPS + c] - 1, 0)
            routed[t, c] = far_rows[lax.rem(entry, fsdp_count) // 2]

    def forward(gathered, chosen, first, parts):
        arrived(gathered, 0)

        @pl.loop(0, chip_count)
        def _(d):
            for e in range(2):
                t = 2 * chip_at(d) + e
                slot = slots[0, far * fsdp_count + t]
                chosen[t] = gathered[slot // (CAPS * own_count), lax.rem(slot, CAPS)]
                push(chosen.at[t], old_rows.at[chip, pl.ds(first, parts)], 4, t, far).start()

    @pl.when(core == 0)
    def _():
        forward(gathered_a, chosen_a, 0, parts_a)

    @pl.when(core == 1)
    def _():
        forward(gathered_b, chosen_b, parts_a, parts_b)

    @pl.loop(1, chip_count)
    def _(d):
        for e in range(2):
            t = 2 * chip_at(d) + e
            push(routed.at[t], routed_in.at[f], 5, t, q).start()

    push(routed.at[sibling], routed_in.at[f], 5, sibling, q).start()
    keep_here(routed.at[f], routed_in.at[f], 5)

    swap.wait()
    block = block_rows[...].reshape(width, width)
    wide = block.astype(F32)
    grad_total = total(wide * wide)

    @pl.when(core == 0)
    def _():
        moment[...] = rows_gram(block)

    @pl.when(core == 1)
    def _():
        moment[...] = columns_gram(block)

    arrived(old_rows, 4)
    on_diagonal = diagonal_mask(side)
    upper = old_rows[...].reshape(len(uppers), side, side)
    trace_value = jnp.zeros((1, 1), F32)
    for b, (rows, columns) in enumerate(uppers):
        old = keep_weight * upper[b].astype(F32)
        fresh = old + fresh_weight * moment[rows, columns]
        moment[rows, columns] = fresh
        if rows == columns:
            trace_value += total(jnp.where(on_diagonal, fresh, 0.0))
        else:
            moment[columns, rows] = jnp.transpose(fresh)
    start = moment[...] * (1.0 / trace_value)
    moment[...] = start
    moment_low[...] = start.astype(BF16)
    inverse[...] = -0.25 * start

    def sweep(step, level):
        low = moment_low[...]
        gap_low[...] = (product(low, low) - 10.0 * moment[...]).astype(BF16)
        mixed = (25.0 * moment[...] + product(gap_low[...], low)) * (1.0 / 16.0)
        mixed_low[...] = mixed.astype(BF16)
        fresh = (25.0 * mixed + product(gap_low[...], mixed_low[...])) * (1.0 / 16.0)
        moment[...] = fresh
        moment_low[...] = fresh.astype(BF16)
        inverse[...] = 1.25 * inverse[...] - 0.25 * (
            level * fresh + product(inverse[...].astype(BF16), moment_low[...])
        )
        return level * 1.25

    level = lax.fori_loop(0, ITERS - 1, sweep, jnp.float32(1.25))
    scale = 1.0 / jnp.sqrt(jnp.sqrt(trace_value))
    root = (jnp.where(diagonal_mask(width), level, 0.0) + inverse[...]) * scale
    roots[core] = root.astype(BF16)
    trade = push(roots.at[core], roots.at[core], 6, sibling, q)
    trade.start()
    trade.wait()

    hidden = product(roots[0], block).astype(BF16)
    shaped = product(hidden, roots[1])
    ratio = jnp.sqrt(grad_total / (total(shaped * shaped) + graft_eps))
    out_rows[...] = (shaped * ratio).astype(BF16).reshape(out_rows.shape)

    @pl.loop(1, chip_count)
    def _(d):
        t = chip_at(d)
        push(out_rows.at[t, core], update_ref.at[chip], 7, 2 * t + core, q).start()

    keep_here(out_rows.at[chip, core], update_ref.at[chip], 7)

    arrived(routed_in, 5)
    for c in range(CAPS):
        entry = table[0, f * CAPS + c]
        used = entry > 0
        odd = lax.rem(lax.max(entry - 1, 0), 2) == 1
        keep = jnp.where(used, keep_weight, 1.0)
        fresh = jnp.where(used, fresh_weight, 0.0)
        fresh_right = jnp.where(odd, fresh, 0.0)
        source = routed_in[:, c].reshape(width, width)
        gram = (fresh - fresh_right) * rows_gram(source) + fresh_right * columns_gram(source)
        old_wide[c] = keep * old_wide[c] + gram
        pltpu.make_async_copy(old_wide.at[c], new_ref.at[c], load_sem.at[c]).start()

    for c in range(CAPS):
        pltpu.make_async_copy(old_wide.at[c], new_ref.at[c], load_sem.at[c]).wait()
    arrived(update_ref, 7)

    @pl.when(core == 0)
    def _():
        left_here(spread_a.at[pl.ds(0, chip_count - 1)], 0)
        left_here(spread_b, 0)
        left_here(chosen_a, 4)

    @pl.when(core == 1)
    def _():
        left_here(spread_a, 0)
        left_here(spread_b.at[pl.ds(0, chip_count - 1)], 0)
        left_here(chosen_b, 4)

    far_push.wait_send()
    left_here(grad_ref.at[pl.ds(0, chip_count - 1)], 2)
    left_here(routed.at[pl.ds(0, fsdp_count - 1)], 5)
    left_here(out_rows.at[pl.ds(0, chip_count - 1), 0], 7)


def body(gradients, old_stats, stat_slot):
    fsdp_count = lax.axis_size("fsdp")
    chip_count = fsdp_count // 2
    blk_count, row_count, width = gradients.shape
    stat_count = stat_slot.shape[0]
    side = width // SPLIT
    parts = SPLIT * (SPLIT + 1) // 2 * (side // row_count) // chip_count
    parts_a, parts_b = parts - parts // 2, parts // 2
    square = (width, width)
    piece = (row_count, side)
    vmem = pltpu.VMEM
    return pl.pallas_call(
        kernel,
        out_shape=(
            jax.ShapeDtypeStruct(gradients.shape, gradients.dtype),
            jax.ShapeDtypeStruct(old_stats.shape, old_stats.dtype),
        ),
        in_specs=[pl.BlockSpec(memory_space=pl.ANY)] * 3,
        out_specs=(pl.BlockSpec(memory_space=pl.ANY), pl.BlockSpec(memory_space=pl.ANY)),
        scratch_shapes=[
            pltpu.SMEM((1, stat_count), jnp.int32),
            vmem((1, stat_count), jnp.int32),
            vmem((1, stat_count), jnp.int32),
            pltpu.SMEM((1, stat_count), jnp.int32),
            vmem((CAPS, *square), F32),
            vmem((chip_count, CAPS, parts_a, *piece), BF16),
            vmem((chip_count, CAPS, parts_b, *piece), BF16),
            vmem((fsdp_count, CAPS, parts_a, *piece), BF16),
            vmem((fsdp_count, CAPS, parts_b, *piece), BF16),
            vmem((fsdp_count, parts_a, *piece), BF16),
            vmem((fsdp_count, parts_b, *piece), BF16),
            vmem((chip_count, parts, *piece), BF16),
            vmem((blk_count, row_count, width), BF16),
            vmem((chip_count, 2, row_count, width), BF16),
            vmem((fsdp_count, CAPS, row_count, width), BF16),
            vmem((fsdp_count, CAPS, row_count, width), BF16),
            vmem((2, *square), BF16),
            vmem(square, F32),
            vmem(square, BF16),
            vmem(square, BF16),
            vmem(square, BF16),
            vmem(square, F32),
            vmem((chip_count, 2, row_count, width), BF16),
            pltpu.SemaphoreType.DMA((CAPS,)),
            pltpu.SemaphoreType.DMA((2,)),
            pltpu.SemaphoreType.DMA((8,)),
            pltpu.SemaphoreType.DMA((8,)),
        ],
        compiler_params=pltpu.CompilerParams(
            collective_id=0, has_side_effects=True, vmem_limit_bytes=60 * 2**20
        ),
        cost_estimate=pl.CostEstimate(
            flops=60 * width**3, bytes_accessed=5 * 2**20, transcendentals=0
        ),
    )(stat_slot.reshape(1, stat_count), gradients, old_stats)


def solution(mesh):
    return jax.shard_map(
        body,
        mesh=mesh,
        in_specs=(P("own", "fsdp", None), P(("fsdp", "own"), None, None), P()),
        out_specs=(P("own", "fsdp", None), P(("fsdp", "own"), None, None)),
        check_vma=False,
    )
```

time: 71.9 us -> 60.2 us (0.84)
  Pallas kernels: 65 us -> 54.6 us
  other arithmetic: 0.84 us -> 0 us
    pallas_call x1, Pallas kernels: 65 us -> 54.6 us  [body(): pl.pallas_call(kernel, out_shape=(jax.ShapeDtypeStruct(gradients.shape, g...]
    add x1 -> x0, other arithmetic: 0.74 us -> none  [body(): places = slots // (CAPS * own_count) * CAPS + slots % CAPS]
    unnamed x8 -> x2, local copies, waits for them, and re-layouts: 5.21 us -> 4.75 us
where the time goes in v2:
time: 60.2 us; the launch traced here: 60 us
  Pallas kernels  54.6 us (91%)
  local copies, waits for them, and re-layouts  4.75 us (8%)
  between operations  0.64 us (1%)
    pallas_call x1, Pallas kernels, body(): pl.pallas_call(kernel, out_shape=(jax.ShapeDtypeStruct(gradients.shape, g...  54.6 us
    unnamed x2, local copies, waits for them, and re-layouts  4.75 us

profile of v2, /device:TPU:1, one launch (start us, length us, event | category | flops | bytes accessed | tf_op | source)
XLA Modules:
  0.0 60.0 jit_solution(7971971281090364539)
XLA Ops:
  0.6 54.6 %shard_map.50 = (bf16[16,16,512]{2,1,0:T(8,128)(2,1)}, f32[2,512,512]{2,1,0:T(8,128)}) custom-call(s32[1,128]{1,0:T(1,128)} %bitcast.1, bf16[16,16,512]{2,1,0:T(8,128)(2,1)} %grad_ref.1, f32[2,512,512]{2,1,0:T(8,128)} %old_ref.1), custom_call_target="tpu_custom_call" | custom-call | flops 8053063680 | bytes 5242880 | tf_op jit(solution)/shard_map/pallas_call | solution.py:329
  55.2 1.7 %copy.7 = bf16[16,16,512]{2,1,0:T(8,128)(2,1)} copy(bf16[16,16,512]{2,1,0:T(8,128)(2,1)} %get-tuple-element.4) | data formatting | bytes 524288
  56.9 3.1 %copy.8 = f32[2,512,512]{2,1,0:T(8,128)} copy(f32[2,512,512]{2,1,0:T(8,128)} %get-tuple-element.5) | data formatting | bytes 4194304

commit v3 on v2

--- a/solution.py
+++ b/solution.py
@@ -290,11 +290,8 @@
         fresh_right = jnp.where(odd, fresh, 0.0)
         source = routed_in[:, c].reshape(width, width)
         gram = (fresh - fresh_right) * rows_gram(source) + fresh_right * columns_gram(source)
-        old_wide[c] = keep * old_wide[c] + gram
-        pltpu.make_async_copy(old_wide.at[c], new_ref.at[c], load_sem.at[c]).start()
-
-    for c in range(CAPS):
-        pltpu.make_async_copy(old_wide.at[c], new_ref.at[c], load_sem.at[c]).wait()
+        new_ref[c] = keep * old_wide[c] + gram
+
     arrived(update_ref, 7)
 
     @pl.when(core == 0)
@@ -313,6 +310,16 @@
     left_here(grad_ref.at[pl.ds(0, chip_count - 1)], 2)
     left_here(routed.at[pl.ds(0, fsdp_count - 1)], 5)
     left_here(out_rows.at[pl.ds(0, chip_count - 1), 0], 7)
+
+
+def write_out(update_ref, stats_ref, update_out, stats_out, sems):
+    copies = [pltpu.make_async_copy(update_ref, update_out, sems.at[CAPS])]
+    for c in range(CAPS):
+        copies.append(pltpu.make_async_copy(stats_ref.at[c], stats_out.at[c], sems.at[c]))
+    for copy in copies:
+        copy.start()
+    for copy in copies:
+        copy.wait()
 
 
 def body(gradients, old_stats, stat_slot):
@@ -326,14 +333,14 @@
     square = (width, width)
     piece = (row_count, side)
     vmem = pltpu.VMEM
-    return pl.pallas_call(
+    update, new_stats = pl.pallas_call(
         kernel,
         out_shape=(
-            jax.ShapeDtypeStruct(gradients.shape, gradients.dtype),
-            jax.ShapeDtypeStruct(old_stats.shape, old_stats.dtype),
+            pltpu.VMEM(gradients.shape, gradients.dtype),
+            pltpu.VMEM(old_stats.shape, old_stats.dtype),
         ),
-        in_specs=[pl.BlockSpec(memory_space=pl.ANY)] * 3,
-        out_specs=(pl.BlockSpec(memory_space=pl.ANY), pl.BlockSpec(memory_space=pl.ANY)),
+        in_specs=[pl.BlockSpec(memory_space=pltpu.HBM)] * 3,
+        out_specs=(pl.BlockSpec(memory_space=pl.ANY), pl.BlockSpec(memory_space=pltpu.VMEM)),
         scratch_shapes=[
             pltpu.SMEM((1, stat_count), jnp.int32),
             vmem((1, stat_count), jnp.int32),
@@ -364,12 +371,23 @@
             pltpu.SemaphoreType.DMA((8,)),
         ],
         compiler_params=pltpu.CompilerParams(
-            collective_id=0, has_side_effects=True, vmem_limit_bytes=60 * 2**20
+            collective_id=0, has_side_effects=True, vmem_limit_bytes=57 * 2**20
         ),
         cost_estimate=pl.CostEstimate(
             flops=60 * width**3, bytes_accessed=5 * 2**20, transcendentals=0
         ),
     )(stat_slot.reshape(1, stat_count), gradients, old_stats)
+    return pl.pallas_call(
+        write_out,
+        out_shape=(
+            jax.ShapeDtypeStruct(gradients.shape, gradients.dtype),
+            jax.ShapeDtypeStruct(old_stats.shape, old_stats.dtype),
+        ),
+        in_specs=[pl.BlockSpec(memory_space=pltpu.VMEM)] * 2,
+        out_specs=(pl.BlockSpec(memory_space=pltpu.HBM), pl.BlockSpec(memory_space=pltpu.HBM)),
+        scratch_shapes=[pltpu.SemaphoreType.DMA((1 + CAPS,))],
+        compiler_params=pltpu.CompilerParams(vmem_limit_bytes=2**20),
+    )(update, new_stats)
 
 
 def solution(mesh):

time: 60.2 us -> 56.7 us (0.942)
  local copies, waits for them, and re-layouts: 4.75 us -> 0 us
  Pallas kernels: 54.6 us -> 55.9 us
    unnamed x2 -> x0, local copies, waits for them, and re-layouts: 4.75 us -> none
    pallas_call x1 -> x2, Pallas kernels: 54.6 us -> 55.9 us  [the longest x1 54.5 us: body(): pl.pallas_call(kernel, out_shape=(pltpu.VMEM(gradients.shape, gradients.d...]
where the time goes in v3:
time: 56.7 us; the launch traced here: 56.5 us
  Pallas kernels  55.9 us (99%)
  between operations  0.64 us (1%)
    pallas_call x1, Pallas kernels, body(): pl.pallas_call(kernel, out_shape=(pltpu.VMEM(gradients.shape, gradients.d...  54.5 us
    pallas_call x1, Pallas kernels, body(): pl.pallas_call(write_out, out_shape=(jax.ShapeDtypeStruct(gradients.shape...  1.43 us

profile of v3, /device:TPU:1, one launch (start us, length us, event | category | flops | bytes accessed | tf_op | source)
XLA Modules:
  0.0 56.5 jit_solution(1398994996661772206)
XLA Ops:
  0.6 54.5 %shard_map.50 = (bf16[16,16,512]{2,1,0:T(8,128)(2,1)S(1)}, f32[2,512,512]{2,1,0:T(8,128)S(1)}) custom-call(s32[1,128]{1,0:T(1,128)} %bitcast.1, bf16[16,16,512]{2,1,0:T(8,128)(2,1)} %grad_ref.1, f32[2,512,512]{2,1,0:T(8,128)} %old_ref.1), custom_call_target="tpu_custom_call" | custom-call | flops 8053063680 | bytes 5242880 | tf_op jit(solution)/shard_map/pallas_call | solution.py:336
  55.1 1.4 %shard_map.51 = (bf16[16,16,512]{2,1,0:T(8,128)(2,1)}, f32[2,512,512]{2,1,0:T(8,128)}) custom-call(bf16[16,16,512]{2,1,0:T(8,128)(2,1)S(1)} %get-tuple-element.4.update_ref, f32[2,512,512]{2,1,0:T(8,128)S(1)} %get-tuple-element.5.stats_ref), custom_call_target="tpu_custom_call" | custom-call | tf_op jit(solution)/shard_map/pallas_call | solution.py:380

commit v4 on v3

--- a/solution.py
+++ b/solution.py
@@ -10,6 +10,7 @@
 ITERS = 6
 CAPS = 2
 SPLIT = 4
+EARLY = 4
 
 keep_weight = 0.9
 fresh_weight = 0.1
@@ -177,17 +178,7 @@
     table_copy.start()
     table_copy.wait()
 
-    arrived(block_rows.at[:, core], 2)
-    swap = push(block_rows.at[:, core], block_rows.at[:, core], 3, sibling, q)
-    swap.start()
-
     far_push.wait_recv()
-
-    @pl.loop(0, fsdp_count)
-    def _(t):
-        for c in range(CAPS):
-            entry = lax.max(table[0, t * CAPS + c] - 1, 0)
-            routed[t, c] = far_rows[lax.rem(entry, fsdp_count) // 2]
 
     def forward(gathered, chosen, first, parts):
         arrived(gathered, 0)
@@ -208,12 +199,24 @@
     def _():
         forward(gathered_b, chosen_b, parts_a, parts_b)
 
-    @pl.loop(1, chip_count)
-    def _(d):
-        for e in range(2):
-            t = 2 * chip_at(d) + e
-            push(routed.at[t], routed_in.at[f], 5, t, q).start()
-
+    arrived(block_rows.at[:, core], 2)
+    swap = push(block_rows.at[:, core], block_rows.at[:, core], 3, sibling, q)
+    swap.start()
+
+    @pl.loop(0, fsdp_count)
+    def _(t):
+        for c in range(CAPS):
+            entry = lax.max(table[0, t * CAPS + c] - 1, 0)
+            routed[t, c] = far_rows[lax.rem(entry, fsdp_count) // 2]
+
+    def route(first, last):
+        @pl.loop(first, last)
+        def _(d):
+            for e in range(2):
+                t = 2 * chip_at(d) + e
+                push(routed.at[t], routed_in.at[f], 5, t, q).start()
+
+    route(1, 1 + EARLY)
     push(routed.at[sibling], routed_in.at[f], 5, sibling, q).start()
     keep_here(routed.at[f], routed_in.at[f], 5)
 
@@ -231,6 +234,7 @@
         moment[...] = columns_gram(block)
 
     arrived(old_rows, 4)
+    route(1 + EARLY, chip_count)
     on_diagonal = diagonal_mask(side)
     upper = old_rows[...].reshape(len(uppers), side, side)
     trace_value = jnp.zeros((1, 1), F32)

time: 56.7 us -> 48.3 us (0.85)
  Pallas kernels: 55.9 us -> 47.5 us
    pallas_call x1, Pallas kernels: 54.5 us -> 46.1 us  [body(): pl.pallas_call(kernel, out_shape=(pltpu.VMEM(gradients.shape, gradients.d...]
where the time goes in v4:
time: 48.3 us; the launch traced here: 48.2 us
  Pallas kernels  47.5 us (98%)
  between operations  0.64 us (1%)
    pallas_call x1, Pallas kernels, body(): pl.pallas_call(kernel, out_shape=(pltpu.VMEM(gradients.shape, gradients.d...  46.1 us
    pallas_call x1, Pallas kernels, body(): pl.pallas_call(write_out, out_shape=(jax.ShapeDtypeStruct(gradients.shape...  1.43 us

profile of v4, /device:TPU:1, one launch (start us, length us, event | category | flops | bytes accessed | tf_op | source)
XLA Modules:
  0.0 48.2 jit_solution(13564855978499036449)
XLA Ops:
  0.6 46.1 %shard_map.50 = (bf16[16,16,512]{2,1,0:T(8,128)(2,1)S(1)}, f32[2,512,512]{2,1,0:T(8,128)S(1)}) custom-call(s32[1,128]{1,0:T(1,128)} %bitcast.1, bf16[16,16,512]{2,1,0:T(8,128)(2,1)} %grad_ref.1, f32[2,512,512]{2,1,0:T(8,128)} %old_ref.1), custom_call_target="tpu_custom_call" | custom-call | flops 8053063680 | bytes 5242880 | tf_op jit(solution)/shard_map/pallas_call | solution.py:340
  46.7 1.4 %shard_map.51 = (bf16[16,16,512]{2,1,0:T(8,128)(2,1)}, f32[2,512,512]{2,1,0:T(8,128)}) custom-call(bf16[16,16,512]{2,1,0:T(8,128)(2,1)S(1)} %get-tuple-element.4.update_ref, f32[2,512,512]{2,1,0:T(8,128)S(1)} %get-tuple-element.5.stats_ref), custom_call_target="tpu_custom_call" | custom-call | tf_op jit(solution)/shard_map/pallas_call | solution.py:384

commit v5 on v4

--- a/solution.py
+++ b/solution.py
@@ -1,3 +1,4 @@
+import functools
 import math
 
 import jax
@@ -10,7 +11,10 @@
 ITERS = 6
 CAPS = 2
 SPLIT = 4
-EARLY = 4
+EARLY = 2
+PLACES = [(0, 0, 0), (0, 0, 1), (0, 1, 0), (1, 0, 0), (1, 1, 0)]
+STAGES = 2
+FIRST = [0, 8]
 
 keep_weight = 0.9
 fresh_weight = 0.1
@@ -52,12 +56,12 @@
     slot_ref, grad_ref, old_ref,
     update_ref, new_ref,
     slots, slot_row, table_row, table,
-    old_wide, spread_a, spread_b, gathered_a, gathered_b, chosen_a, chosen_b, old_rows,
-    far_rows, block_rows, routed, routed_in, roots,
+    old_wide, spread, gathered, chosen, old_rows,
+    grads, far_rows, block_rows, routed, routed_in, roots,
     moment, moment_low, gap_low, mixed_low, inverse, out_rows,
-    load_sem, small_sem, send_sems, recv_sems,
+    load_sem, small_sem, entered, send_sems, recv_sems,
 ):
-    chip_count = spread_a.shape[0]
+    chip_count = spread[0][0].shape[0]
     fsdp_count = 2 * chip_count
     chip_side = math.isqrt(chip_count)
     own_count = lax.axis_size("own")
@@ -69,8 +73,6 @@
     core = lax.rem(f, 2)
     chip = f // 2
     sibling = f + 1 - 2 * core
-    parts_a = spread_a.shape[2]
-    parts_b = spread_b.shape[2]
 
     def chip_at(d):
         turn = lax.rem(5 * d, chip_count)
@@ -104,7 +106,8 @@
         pltpu.make_async_copy(slot_ref, slots, small_sem.at[0]),
         pltpu.make_async_copy(slot_ref, slot_row, small_sem.at[1]),
     ]
-    for load in loads + slot_loads:
+    grad_load = pltpu.make_async_copy(grad_ref, grads, small_sem.at[2])
+    for load in [*loads, grad_load, *slot_loads]:
         load.start()
 
     barrier = pltpu.get_barrier_semaphore()
@@ -127,43 +130,37 @@
         for b, (rows, columns) in enumerate(uppers):
             low = old_wide[c, rows, columns].astype(BF16).reshape(pieces, row_count, side)
             for piece in range(pieces):
-                target, part = divmod(b * pieces + piece, parts_a + parts_b)
-                if part < parts_a:
-                    spread_a[target, c, part] = low[piece]
-                else:
-                    spread_b[target, c, part - parts_a] = low[piece]
-
+                target, part = divmod(b * pieces + piece, len(PLACES))
+                stage, e, at = PLACES[part]
+                spread[stage][e][target, c, at] = low[piece]
+
+    grad_load.wait()
     pl.semaphore_wait(barrier, fsdp_count)
-
-    far_push = push(grad_ref, far_rows, 1, f, far)
+    pl.semaphore_signal(
+        entered, inc=1, device_id={"fsdp": f, "own": far}, device_id_type=MESH
+    )
+
+    far_push = push(grads, far_rows, 1, f, far)
     far_push.start()
 
-    def spread_to(source, target, e):
+    def spread_to(stage, e):
+        source, target = spread[stage][e], gathered[stage][e]
+
         @pl.loop(1, chip_count)
         def _(d):
             t = chip_at(d)
-            push(source.at[t], target.at[f], 0, 2 * t + e, q).start()
-
-    @pl.when(core == 0)
-    def _():
-        spread_to(spread_a, gathered_a, 0)
-        spread_to(spread_b, gathered_b, 1)
-        push(spread_b.at[chip], gathered_b.at[f], 0, sibling, q).start()
-        keep_here(spread_a.at[chip], gathered_a.at[f], 0)
-
-    @pl.when(core == 1)
-    def _():
-        spread_to(spread_b, gathered_b, 1)
-        spread_to(spread_a, gathered_a, 0)
-        push(spread_a.at[chip], gathered_a.at[f], 0, sibling, q).start()
-        keep_here(spread_b.at[chip], gathered_b.at[f], 0)
-
-    @pl.loop(1, chip_count)
-    def _(d):
-        t = chip_at(d)
-        push(grad_ref.at[t], block_rows.at[chip, core], 2, 2 * t + core, q).start()
-
-    keep_here(grad_ref.at[chip], block_rows.at[chip, core], 2)
+            push(source.at[t], target.at[f], FIRST[stage], 2 * t + e, q).start()
+
+    def spread_stage(stage, e):
+        spread_to(stage, e)
+        spread_to(stage, 1 - e)
+        other = gathered[stage][1 - e]
+        push(spread[stage][1 - e].at[chip], other.at[f], FIRST[stage], sibling, q).start()
+        keep_here(spread[stage][e].at[chip], gathered[stage][e].at[f], FIRST[stage])
+
+    for stage in range(STAGES):
+        for e in range(2):
+            pl.when(core == e)(functools.partial(spread_stage, stage, e))
 
     for load in slot_loads:
         load.wait()
@@ -178,30 +175,37 @@
     table_copy.start()
     table_copy.wait()
 
-    far_push.wait_recv()
-
-    def forward(gathered, chosen, first, parts):
-        arrived(gathered, 0)
+    pl.semaphore_wait(entered, 1)
+
+    def forward(stage, e):
+        source, picked = gathered[stage][e], chosen[stage][e]
+        first, parts = PLACES.index((stage, e, 0)), picked.shape[1]
+        arrived(source, FIRST[stage])
 
         @pl.loop(0, chip_count)
         def _(d):
-            for e in range(2):
-                t = 2 * chip_at(d) + e
+            for side_core in range(2):
+                t = 2 * chip_at(d) + side_core
                 slot = slots[0, far * fsdp_count + t]
-                chosen[t] = gathered[slot // (CAPS * own_count), lax.rem(slot, CAPS)]
-                push(chosen.at[t], old_rows.at[chip, pl.ds(first, parts)], 4, t, far).start()
-
-    @pl.when(core == 0)
-    def _():
-        forward(gathered_a, chosen_a, 0, parts_a)
-
-    @pl.when(core == 1)
-    def _():
-        forward(gathered_b, chosen_b, parts_a, parts_b)
+                picked[t] = source[slot // (CAPS * own_count), lax.rem(slot, CAPS)]
+                push(picked.at[t], old_rows.at[chip, pl.ds(first, parts)], 4, t, far).start()
+
+    for stage in range(STAGES):
+        for e in range(2):
+            pl.when(core == e)(functools.partial(forward, stage, e))
+
+    @pl.loop(1, chip_count)
+    def _(d):
+        t = chip_at(d)
+        push(grads.at[t], block_rows.at[chip, core], 2, 2 * t + core, q).start()
+
+    keep_here(grads.at[chip], block_rows.at[chip, core], 2)
 
     arrived(block_rows.at[:, core], 2)
     swap = push(block_rows.at[:, core], block_rows.at[:, core], 3, sibling, q)
     swap.start()
+
+    far_push.wait_recv()
 
     @pl.loop(0, fsdp_count)
     def _(t):
@@ -298,20 +302,17 @@
 
     arrived(update_ref, 7)
 
-    @pl.when(core == 0)
-    def _():
-        left_here(spread_a.at[pl.ds(0, chip_count - 1)], 0)
-        left_here(spread_b, 0)
-        left_here(chosen_a, 4)
-
-    @pl.when(core == 1)
-    def _():
-        left_here(spread_a, 0)
-        left_here(spread_b.at[pl.ds(0, chip_count - 1)], 0)
-        left_here(chosen_b, 4)
+    def all_left(stage, e):
+        left_here(spread[stage][e].at[pl.ds(0, chip_count - 1)], FIRST[stage])
+        left_here(spread[stage][1 - e], FIRST[stage])
+        left_here(chosen[stage][e], 4)
+
+    for stage in range(STAGES):
+        for e in range(2):
+            pl.when(core == e)(functools.partial(all_left, stage, e))
 
     far_push.wait_send()
-    left_here(grad_ref.at[pl.ds(0, chip_count - 1)], 2)
+    left_here(grads.at[pl.ds(0, chip_count - 1)], 2)
     left_here(routed.at[pl.ds(0, fsdp_count - 1)], 5)
     left_here(out_rows.at[pl.ds(0, chip_count - 1), 0], 7)
 
@@ -332,11 +333,17 @@
     blk_count, row_count, width = gradients.shape
     stat_count = stat_slot.shape[0]
     side = width // SPLIT
-    parts = SPLIT * (SPLIT + 1) // 2 * (side // row_count) // chip_count
-    parts_a, parts_b = parts - parts // 2, parts // 2
     square = (width, width)
     piece = (row_count, side)
     vmem = pltpu.VMEM
+
+    def staged(*lead):
+        def of(stage, e):
+            parts = sum(place[:2] == (stage, e) for place in PLACES)
+            return vmem((*lead, parts, *piece), BF16)
+
+        return [[of(stage, e) for e in range(2)] for stage in range(STAGES)]
+
     update, new_stats = pl.pallas_call(
         kernel,
         out_shape=(
@@ -351,13 +358,11 @@
             vmem((1, stat_count), jnp.int32),
             pltpu.SMEM((1, stat_count), jnp.int32),
             vmem((CAPS, *square), F32),
-            vmem((chip_count, CAPS, parts_a, *piece), BF16),
-            vmem((chip_count, CAPS, parts_b, *piece), BF16),
-            vmem((fsdp_count, CAPS, parts_a, *piece), BF16),
-            vmem((fsdp_count, CAPS, parts_b, *piece), BF16),
-            vmem((fsdp_count, parts_a, *piece), BF16),
-            vmem((fsdp_count, parts_b, *piece), BF16),
-            vmem((chip_count, parts, *piece), BF16),
+            staged(chip_count, CAPS),
+            staged(fsdp_count, CAPS),
+            staged(fsdp_count),
+            vmem((chip_count, len(PLACES), *piece), BF16),
+            vmem((blk_count, row_count, width), BF16),
             vmem((blk_count, row_count, width), BF16),
             vmem((chip_count, 2, row_count, width), BF16),
             vmem((fsdp_count, CAPS, row_count, width), BF16),
@@ -370,9 +375,10 @@
             vmem(square, F32),
             vmem((chip_count, 2, row_count, width), BF16),
             pltpu.SemaphoreType.DMA((CAPS,)),
-            pltpu.SemaphoreType.DMA((2,)),
-            pltpu.SemaphoreType.DMA((8,)),
-            pltpu.SemaphoreType.DMA((8,)),
+            pltpu.SemaphoreType.DMA((3,)),
+            pltpu.SemaphoreType.REGULAR,
+            pltpu.SemaphoreType.DMA((9,)),
+            pltpu.SemaphoreType.DMA((9,)),
         ],
         compiler_params=pltpu.CompilerParams(
             collective_id=0, has_side_effects=True, vmem_limit_bytes=57 * 2**20

time: 48.3 us -> 46.8 us (0.969)
  Pallas kernels: 47.5 us -> 46 us
    pallas_call x1, Pallas kernels: 46.1 us -> 44.5 us  [body(): pl.pallas_call(kernel, out_shape=(pltpu.VMEM(gradients.shape, gradients.d...]
where the time goes in v5:
time: 46.8 us; the launch traced here: 46.6 us
  Pallas kernels  46 us (98%)
  between operations  0.64 us (1%)
    pallas_call x1, Pallas kernels, body(): pl.pallas_call(kernel, out_shape=(pltpu.VMEM(gradients.shape, gradients.d...  44.5 us
    pallas_call x1, Pallas kernels, body(): pl.pallas_call(write_out, out_shape=(jax.ShapeDtypeStruct(gradients.shape...  1.43 us

profile of v5, /device:TPU:1, one launch (start us, length us, event | category | flops | bytes accessed | tf_op | source)
XLA Modules:
  0.0 46.6 jit_solution(3078839324978553506)
XLA Ops:
  0.6 44.5 %shard_map.50 = (bf16[16,16,512]{2,1,0:T(8,128)(2,1)S(1)}, f32[2,512,512]{2,1,0:T(8,128)S(1)}) custom-call(s32[1,128]{1,0:T(1,128)} %bitcast.1, bf16[16,16,512]{2,1,0:T(8,128)(2,1)} %grad_ref.1, f32[2,512,512]{2,1,0:T(8,128)} %old_ref.1), custom_call_target="tpu_custom_call" | custom-call | flops 8053063680 | bytes 5242880 | tf_op jit(solution)/shard_map/pallas_call | solution.py:347
  45.2 1.4 %shard_map.51 = (bf16[16,16,512]{2,1,0:T(8,128)(2,1)}, f32[2,512,512]{2,1,0:T(8,128)}) custom-call(bf16[16,16,512]{2,1,0:T(8,128)(2,1)S(1)} %get-tuple-element.4.update_ref, f32[2,512,512]{2,1,0:T(8,128)S(1)} %get-tuple-element.5.stats_ref), custom_call_target="tpu_custom_call" | custom-call | tf_op jit(solution)/shard_map/pallas_call | solution.py:390

commit v6 on v5

--- a/solution.py
+++ b/solution.py
@@ -11,7 +11,7 @@
 ITERS = 6
 CAPS = 2
 SPLIT = 4
-EARLY = 2
+EARLY = 4
 PLACES = [(0, 0, 0), (0, 0, 1), (0, 1, 0), (1, 0, 0), (1, 1, 0)]
 STAGES = 2
 FIRST = [0, 8]
@@ -57,8 +57,8 @@
     update_ref, new_ref,
     slots, slot_row, table_row, table,
     old_wide, spread, gathered, chosen, old_rows,
-    grads, far_rows, block_rows, routed, routed_in, roots,
-    moment, moment_low, gap_low, mixed_low, inverse, out_rows,
+    grads, far_rows, block_rows, block_all, routed, routed_in, roots,
+    moment, moment_low, gap_low, mixed, mixed_low, inverse, inverse_low, out_rows,
     load_sem, small_sem, entered, send_sems, recv_sems,
 ):
     chip_count = spread[0][0].shape[0]
@@ -225,7 +225,8 @@
     keep_here(routed.at[f], routed_in.at[f], 5)
 
     swap.wait()
-    block = block_rows[...].reshape(width, width)
+    block_all[...] = block_rows[...].reshape(width, width)
+    block = block_all[...]
     wide = block.astype(F32)
     grad_total = total(wide * wide)
 
@@ -242,44 +243,89 @@
     on_diagonal = diagonal_mask(side)
     upper = old_rows[...].reshape(len(uppers), side, side)
     trace_value = jnp.zeros((1, 1), F32)
+    half = width // 2
+    left_half, right_half = pl.ds(0, half), pl.ds(half, half)
+    bands = [pl.ds(b * side, side) for b in range(SPLIT)]
+    tiles = [(band, right_half) for band in bands[:2]]
+    tiles += [(band, left_half) for band in bands[:2]]
+    tiles += [(band, right_half) for band in bands[2:]]
+
+    def put(ref, rows, columns, values):
+        rounded = values.astype(BF16)
+        ref[rows, columns] = rounded
+        if rows.start < half and columns.start == half:
+            ref[columns, rows] = jnp.transpose(rounded)
+
     for b, (rows, columns) in enumerate(uppers):
         old = keep_weight * upper[b].astype(F32)
         fresh = old + fresh_weight * moment[rows, columns]
         moment[rows, columns] = fresh
         if rows == columns:
             trace_value += total(jnp.where(on_diagonal, fresh, 0.0))
-        else:
+        elif rows.start // half == columns.start // half:
             moment[columns, rows] = jnp.transpose(fresh)
-    start = moment[...] * (1.0 / trace_value)
-    moment[...] = start
-    moment_low[...] = start.astype(BF16)
-    inverse[...] = -0.25 * start
-
-    def sweep(step, level):
-        low = moment_low[...]
-        gap_low[...] = (product(low, low) - 10.0 * moment[...]).astype(BF16)
-        mixed = (25.0 * moment[...] + product(gap_low[...], low)) * (1.0 / 16.0)
-        mixed_low[...] = mixed.astype(BF16)
-        fresh = (25.0 * mixed + product(gap_low[...], mixed_low[...])) * (1.0 / 16.0)
-        moment[...] = fresh
-        moment_low[...] = fresh.astype(BF16)
-        inverse[...] = 1.25 * inverse[...] - 0.25 * (
-            level * fresh + product(inverse[...].astype(BF16), moment_low[...])
-        )
-        return level * 1.25
-
-    level = lax.fori_loop(0, ITERS - 1, sweep, jnp.float32(1.25))
+    inverse_trace = 1.0 / trace_value
+    for rows, columns in tiles:
+        start = moment[rows, columns] * inverse_trace
+        moment[rows, columns] = start
+        put(moment_low, rows, columns, start)
+        inverse[rows, columns] = -0.25 * start
+        put(inverse_low, rows, columns, -0.25 * start)
+
+    def next_inverse(rows, columns, level):
+        part = product(inverse_low[rows, :], moment_low[:, columns])
+        return 1.25 * inverse[rows, columns] - 0.25 * (level * moment[rows, columns] + part)
+
+    def sweep(with_inverse, step, level):
+        for rows, columns in tiles:
+            square = product(moment_low[rows, :], moment_low[:, columns])
+            put(gap_low, rows, columns, square - 10.0 * moment[rows, columns])
+            if with_inverse:
+                inverse[rows, columns] = next_inverse(rows, columns, level)
+        if with_inverse:
+            for rows, columns in tiles:
+                put(inverse_low, rows, columns, inverse[rows, columns])
+        for rows, columns in tiles:
+            part = product(gap_low[rows, :], moment_low[:, columns])
+            values = (25.0 * moment[rows, columns] + part) * (1.0 / 16.0)
+            mixed[rows, columns] = values
+            put(mixed_low, rows, columns, values)
+        for rows, columns in tiles:
+            part = product(gap_low[rows, :], mixed_low[:, columns])
+            values = (25.0 * mixed[rows, columns] + part) * (1.0 / 16.0)
+            moment[rows, columns] = values
+            put(moment_low, rows, columns, values)
+        return level * 1.25 if with_inverse else level
+
+    sweep(False, 0, None)
+    level = lax.fori_loop(1, ITERS - 1, functools.partial(sweep, True), jnp.float32(1.25))
     scale = 1.0 / jnp.sqrt(jnp.sqrt(trace_value))
-    root = (jnp.where(diagonal_mask(width), level, 0.0) + inverse[...]) * scale
-    roots[core] = root.astype(BF16)
-    trade = push(roots.at[core], roots.at[core], 6, sibling, q)
+    own_root = roots.at[core]
+    for rows, columns in tiles:
+        root = next_inverse(rows, columns, level)
+        if rows.start // half == columns.start // half:
+            spots = [
+                lax.broadcasted_iota(jnp.int32, (side, half), dim) for dim in range(2)
+            ]
+            diagonal = spots[1] - spots[0] == rows.start - columns.start
+            root += jnp.where(diagonal, 1.25 * level, 0.0)
+        put(own_root, rows, columns, root * scale)
+    trade = push(own_root, own_root, 6, sibling, q)
     trade.start()
-    trade.wait()
-
-    hidden = product(roots[0], block).astype(BF16)
-    shaped = product(hidden, roots[1])
-    ratio = jnp.sqrt(grad_total / (total(shaped * shaped) + graft_eps))
-    out_rows[...] = (shaped * ratio).astype(BF16).reshape(out_rows.shape)
+
+    pl.when(core == 1)(trade.wait_recv)
+    quarters = [(rows, columns) for columns in (left_half, right_half) for rows in (left_half, right_half)]
+    for rows, columns in quarters:
+        hidden = product(roots[0, rows, :], block_all[:, columns])
+        gap_low[rows, columns] = hidden.astype(BF16)
+    pl.when(core == 0)(trade.wait_recv)
+    shaped_total = jnp.zeros((1, 1), F32)
+    for rows, columns in quarters:
+        shaped = product(gap_low[rows, :], roots[1, :, columns])
+        mixed[rows, columns] = shaped
+        shaped_total += total(shaped * shaped)
+    ratio = jnp.sqrt(grad_total / (shaped_total + graft_eps))
+    out_rows[...] = (mixed[...] * ratio).astype(BF16).reshape(out_rows.shape)
 
     @pl.loop(1, chip_count)
     def _(d):
@@ -314,6 +360,7 @@
     far_push.wait_send()
     left_here(grads.at[pl.ds(0, chip_count - 1)], 2)
     left_here(routed.at[pl.ds(0, fsdp_count - 1)], 5)
+    trade.wait_send()
     left_here(out_rows.at[pl.ds(0, chip_count - 1), 0], 7)
 
 
@@ -365,14 +412,17 @@
             vmem((blk_count, row_count, width), BF16),
             vmem((blk_count, row_count, width), BF16),
             vmem((chip_count, 2, row_count, width), BF16),
+            vmem(square, BF16),
             vmem((fsdp_count, CAPS, row_count, width), BF16),
             vmem((fsdp_count, CAPS, row_count, width), BF16),
             vmem((2, *square), BF16),
             vmem(square, F32),
             vmem(square, BF16),
             vmem(square, BF16),
+            vmem(square, F32),
             vmem(square, BF16),
             vmem(square, F32),
+            vmem(square, BF16),
             vmem((chip_count, 2, row_count, width), BF16),
             pltpu.SemaphoreType.DMA((CAPS,)),
             pltpu.SemaphoreType.DMA((3,)),

time: 46.8 us -> 46.3 us (0.989)
  Pallas kernels: 46 us -> 45.5 us
    pallas_call x1, Pallas kernels: 44.5 us -> 44.1 us  [body(): pl.pallas_call(kernel, out_shape=(pltpu.VMEM(gradients.shape, gradients.d...]
where the time goes in v6:
time: 46.3 us; the launch traced here: 46.1 us
  Pallas kernels  45.5 us (98%)
  between operations  0.64 us (1%)
    pallas_call x1, Pallas kernels, body(): pl.pallas_call(kernel, out_shape=(pltpu.VMEM(gradients.shape, gradients.d...  44.1 us
    pallas_call x1, Pallas kernels, body(): pl.pallas_call(write_out, out_shape=(jax.ShapeDtypeStruct(gradients.shape...  1.43 us

profile of v6, /device:TPU:1, one launch (start us, length us, event | category | flops | bytes accessed | tf_op | source)
XLA Modules:
  0.0 46.1 jit_solution(475173108692303505)
XLA Ops:
  0.6 44.1 %shard_map.50 = (bf16[16,16,512]{2,1,0:T(8,128)(2,1)S(1)}, f32[2,512,512]{2,1,0:T(8,128)S(1)}) custom-call(s32[1,128]{1,0:T(1,128)} %bitcast.1, bf16[16,16,512]{2,1,0:T(8,128)(2,1)} %grad_ref.1, f32[2,512,512]{2,1,0:T(8,128)} %old_ref.1), custom_call_target="tpu_custom_call" | custom-call | flops 8053063680 | bytes 5242880 | tf_op jit(solution)/shard_map/pallas_call | solution.py:394
  44.7 1.4 %shard_map.51 = (bf16[16,16,512]{2,1,0:T(8,128)(2,1)}, f32[2,512,512]{2,1,0:T(8,128)}) custom-call(bf16[16,16,512]{2,1,0:T(8,128)(2,1)S(1)} %get-tuple-element.4.update_ref, f32[2,512,512]{2,1,0:T(8,128)S(1)} %get-tuple-element.5.stats_ref), custom_call_target="tpu_custom_call" | custom-call | tf_op jit(solution)/shard_map/pallas_call | solution.py:440

commit v7 on v6

--- a/solution.py
+++ b/solution.py
@@ -75,7 +75,7 @@
     sibling = f + 1 - 2 * core
 
     def chip_at(d):
-        turn = lax.rem(5 * d, chip_count)
+        turn = lax.rem(7 * d, chip_count)
         y = lax.rem(chip // chip_side + turn // chip_side, chip_side)
         x = lax.rem(chip + turn, chip_side)
         return y * chip_side + x
@@ -117,7 +117,7 @@
             barrier, inc=1, device_id={"fsdp": row, "own": plane}, device_id_type=MESH
         )
 
-    @pl.loop(1, fsdp_count)
+    @pl.loop(1, fsdp_count, unroll=True)
     def _(d):
         greet(lax.rem(f + d, fsdp_count), q)
 
@@ -146,7 +146,7 @@
     def spread_to(stage, e):
         source, target = spread[stage][e], gathered[stage][e]
 
-        @pl.loop(1, chip_count)
+        @pl.loop(1, chip_count, unroll=True)
         def _(d):
             t = chip_at(d)
             push(source.at[t], target.at[f], FIRST[stage], 2 * t + e, q).start()
@@ -182,7 +182,7 @@
         first, parts = PLACES.index((stage, e, 0)), picked.shape[1]
         arrived(source, FIRST[stage])
 
-        @pl.loop(0, chip_count)
+        @pl.loop(0, chip_count, unroll=4)
         def _(d):
             for side_core in range(2):
                 t = 2 * chip_at(d) + side_core
@@ -190,24 +190,27 @@
                 picked[t] = source[slot // (CAPS * own_count), lax.rem(slot, CAPS)]
                 push(picked.at[t], old_rows.at[chip, pl.ds(first, parts)], 4, t, far).start()
 
-    for stage in range(STAGES):
-        for e in range(2):
-            pl.when(core == e)(functools.partial(forward, stage, e))
-
-    @pl.loop(1, chip_count)
+    for e in range(2):
+        pl.when(core == e)(functools.partial(forward, 0, e))
+
+    @pl.loop(1, chip_count, unroll=True)
     def _(d):
         t = chip_at(d)
         push(grads.at[t], block_rows.at[chip, core], 2, 2 * t + core, q).start()
 
     keep_here(grads.at[chip], block_rows.at[chip, core], 2)
 
+    for stage in range(1, STAGES):
+        for e in range(2):
+            pl.when(core == e)(functools.partial(forward, stage, e))
+
     arrived(block_rows.at[:, core], 2)
     swap = push(block_rows.at[:, core], block_rows.at[:, core], 3, sibling, q)
     swap.start()
 
     far_push.wait_recv()
 
-    @pl.loop(0, fsdp_count)
+    @pl.loop(0, fsdp_count, unroll=4)
     def _(t):
         for c in range(CAPS):
             entry = lax.max(table[0, t * CAPS + c] - 1, 0)
@@ -301,6 +304,10 @@
     level = lax.fori_loop(1, ITERS - 1, functools.partial(sweep, True), jnp.float32(1.25))
     scale = 1.0 / jnp.sqrt(jnp.sqrt(trace_value))
     own_root = roots.at[core]
+
+    def trade_half(rows):
+        push(own_root.at[rows], own_root.at[rows], 6, sibling, q).start()
+
     for rows, columns in tiles:
         root = next_inverse(rows, columns, level)
         if rows.start // half == columns.start // half:
@@ -310,8 +317,10 @@
             diagonal = spots[1] - spots[0] == rows.start - columns.start
             root += jnp.where(diagonal, 1.25 * level, 0.0)
         put(own_root, rows, columns, root * scale)
+        if (rows, columns) == tiles[3]:
+            trade_half(left_half)
     trade = push(own_root, own_root, 6, sibling, q)
-    trade.start()
+    trade_half(right_half)
 
     pl.when(core == 1)(trade.wait_recv)
     quarters = [(rows, columns) for columns in (left_half, right_half) for rows in (left_half, right_half)]
@@ -327,7 +336,7 @@
     ratio = jnp.sqrt(grad_total / (shaped_total + graft_eps))
     out_rows[...] = (mixed[...] * ratio).astype(BF16).reshape(out_rows.shape)
 
-    @pl.loop(1, chip_count)
+    @pl.loop(1, chip_count, unroll=True)
     def _(d):
         t = chip_at(d)
         push(out_rows.at[t, core], update_ref.at[chip], 7, 2 * t + core, q).start()

time: 46.3 us -> 45.6 us (0.985)
  Pallas kernels: 45.5 us -> 44.8 us
    pallas_call x1, Pallas kernels: 44.1 us -> 43.3 us  [body(): pl.pallas_call(kernel, out_shape=(pltpu.VMEM(gradients.shape, gradients.d...]
where the time goes in v7:
time: 45.6 us; the launch traced here: 45.4 us
  Pallas kernels  44.8 us (98%)
  between operations  0.64 us (1%)
    pallas_call x1, Pallas kernels, body(): pl.pallas_call(kernel, out_shape=(pltpu.VMEM(gradients.shape, gradients.d...  43.3 us
    pallas_call x1, Pallas kernels, body(): pl.pallas_call(write_out, out_shape=(jax.ShapeDtypeStruct(gradients.shape...  1.43 us

profile of v7, /device:TPU:1, one launch (start us, length us, event | category | flops | bytes accessed | tf_op | source)
XLA Modules:
  0.0 45.4 jit_solution(18907542567225886)
XLA Ops:
  0.6 43.3 %shard_map.50 = (bf16[16,16,512]{2,1,0:T(8,128)(2,1)S(1)}, f32[2,512,512]{2,1,0:T(8,128)S(1)}) custom-call(s32[1,128]{1,0:T(1,128)} %bitcast.1, bf16[16,16,512]{2,1,0:T(8,128)(2,1)} %grad_ref.1, f32[2,512,512]{2,1,0:T(8,128)} %old_ref.1), custom_call_target="tpu_custom_call" | custom-call | flops 8053063680 | bytes 5242880 | tf_op jit(solution)/shard_map/pallas_call | solution.py:403
  44.0 1.4 %shard_map.51 = (bf16[16,16,512]{2,1,0:T(8,128)(2,1)}, f32[2,512,512]{2,1,0:T(8,128)}) custom-call(bf16[16,16,512]{2,1,0:T(8,128)(2,1)S(1)} %get-tuple-element.4.update_ref, f32[2,512,512]{2,1,0:T(8,128)S(1)} %get-tuple-element.5.stats_ref), custom_call_target="tpu_custom_call" | custom-call | tf_op jit(solution)/shard_map/pallas_call | solution.py:449

commit v8 on v7

--- a/solution.py
+++ b/solution.py
@@ -125,15 +125,19 @@
 
     side, uppers = upper_blocks(width)
     pieces = side // row_count
-    for c in range(CAPS):
-        loads[c].wait()
-        for b, (rows, columns) in enumerate(uppers):
-            low = old_wide[c, rows, columns].astype(BF16).reshape(pieces, row_count, side)
-            for piece in range(pieces):
-                target, part = divmod(b * pieces + piece, len(PLACES))
-                stage, e, at = PLACES[part]
-                spread[stage][e][target, c, at] = low[piece]
-
+    def lay_out(wanted):
+        for c in range(CAPS):
+            for b, (rows, columns) in enumerate(uppers):
+                for piece in range(pieces):
+                    target, part = divmod(b * pieces + piece, len(PLACES))
+                    stage, e, at = PLACES[part]
+                    if stage == wanted:
+                        some = pl.ds(rows.start + piece * row_count, row_count)
+                        spread[stage][e][target, c, at] = old_wide[c, some, columns].astype(BF16)
+
+    for load in loads:
+        load.wait()
+    lay_out(0)
     grad_load.wait()
     pl.semaphore_wait(barrier, fsdp_count)
     pl.semaphore_signal(
@@ -159,6 +163,8 @@
         keep_here(spread[stage][e].at[chip], gathered[stage][e].at[f], FIRST[stage])
 
     for stage in range(STAGES):
+        if stage > 0:
+            lay_out(stage)
         for e in range(2):
             pl.when(core == e)(functools.partial(spread_stage, stage, e))
 

time: 45.6 us -> 45.6 us (level)
  no operation moved by 1% of the time
where the time goes in v8:
time: 45.6 us; the launch traced here: 45.4 us
  Pallas kernels  44.8 us (98%)
  between operations  0.64 us (1%)
    pallas_call x1, Pallas kernels, body(): pl.pallas_call(kernel, out_shape=(pltpu.VMEM(gradients.shape, gradients.d...  43.3 us
    pallas_call x1, Pallas kernels, body(): pl.pallas_call(write_out, out_shape=(jax.ShapeDtypeStruct(gradients.shape...  1.43 us

profile of v8, /device:TPU:1, one launch (start us, length us, event | category | flops | bytes accessed | tf_op | source)
XLA Modules:
  0.0 45.4 jit_solution(12007798195269683542)
XLA Ops:
  0.6 43.3 %shard_map.50 = (bf16[16,16,512]{2,1,0:T(8,128)(2,1)S(1)}, f32[2,512,512]{2,1,0:T(8,128)S(1)}) custom-call(s32[1,128]{1,0:T(1,128)} %bitcast.1, bf16[16,16,512]{2,1,0:T(8,128)(2,1)} %grad_ref.1, f32[2,512,512]{2,1,0:T(8,128)} %old_ref.1), custom_call_target="tpu_custom_call" | custom-call | flops 8053063680 | bytes 5242880 | tf_op jit(solution)/shard_map/pallas_call | solution.py:409
  44.0 1.4 %shard_map.51 = (bf16[16,16,512]{2,1,0:T(8,128)(2,1)}, f32[2,512,512]{2,1,0:T(8,128)}) custom-call(bf16[16,16,512]{2,1,0:T(8,128)(2,1)S(1)} %get-tuple-element.4.update_ref, f32[2,512,512]{2,1,0:T(8,128)S(1)} %get-tuple-element.5.stats_ref), custom_call_target="tpu_custom_call" | custom-call | tf_op jit(solution)/shard_map/pallas_call | solution.py:455

commit v9 on v7

--- a/solution.py
+++ b/solution.py
@@ -11,7 +11,7 @@
 ITERS = 6
 CAPS = 2
 SPLIT = 4
-EARLY = 4
+EARLY = 6
 PLACES = [(0, 0, 0), (0, 0, 1), (0, 1, 0), (1, 0, 0), (1, 1, 0)]
 STAGES = 2
 FIRST = [0, 8]

time: 45.6 us -> 45.5 us (level)
  no operation moved by 1% of the time
where the time goes in v9:
time: 45.5 us; the launch traced here: 45.3 us
  Pallas kernels  44.7 us (98%)
  between operations  0.64 us (1%)
    pallas_call x1, Pallas kernels, body(): pl.pallas_call(kernel, out_shape=(pltpu.VMEM(gradients.shape, gradients.d...  43.3 us
    pallas_call x1, Pallas kernels, body(): pl.pallas_call(write_out, out_shape=(jax.ShapeDtypeStruct(gradients.shape...  1.43 us

profile of v9, /device:TPU:1, one launch (start us, length us, event | category | flops | bytes accessed | tf_op | source)
XLA Modules:
  0.0 45.3 jit_solution(5464818657755995594)
XLA Ops:
  0.6 43.3 %shard_map.50 = (bf16[16,16,512]{2,1,0:T(8,128)(2,1)S(1)}, f32[2,512,512]{2,1,0:T(8,128)S(1)}) custom-call(s32[1,128]{1,0:T(1,128)} %bitcast.1, bf16[16,16,512]{2,1,0:T(8,128)(2,1)} %grad_ref.1, f32[2,512,512]{2,1,0:T(8,128)} %old_ref.1), custom_call_target="tpu_custom_call" | custom-call | flops 8053063680 | bytes 5242880 | tf_op jit(solution)/shard_map/pallas_call | solution.py:403
  43.9 1.4 %shard_map.51 = (bf16[16,16,512]{2,1,0:T(8,128)(2,1)}, f32[2,512,512]{2,1,0:T(8,128)}) custom-call(bf16[16,16,512]{2,1,0:T(8,128)(2,1)S(1)} %get-tuple-element.4.update_ref, f32[2,512,512]{2,1,0:T(8,128)S(1)} %get-tuple-element.5.stats_ref), custom_call_target="tpu_custom_call" | custom-call | tf_op jit(solution)/shard_map/pallas_call | solution.py:449
